TPU v7x, 32 devices: a whole 2x2x4 slice. The times are simulated.
32 devices in a mesh: groups: 2 (over y), segment: 4 (over x, core), space: 4 (over z).
Axes of the slice: x: 2, y: 2, z: 4, core: 2. Of those that a mesh axis runs over, the one named last changes fastest.
Arguments:
- inputs: bfloat16 [4, 32, 8, 256], P('groups', 'space'), parts along dimension 0, may hold values from -6 to 6
- cotangent: bfloat16 [4, 32, 256], P('groups', 'space'), parts along dimension 0, may hold values from -6 to 6
- lift_weight: bfloat16 [8, 64], replicated, may hold values from -2 to 2
- lift_bias: float32 [64], replicated, may hold values from -3 to 3
- point_weight: bfloat16 [4, 64, 64], P('segment'), may hold values from -0.75 to 0.75
- layer_bias: float32 [4, 64], P('segment'), may hold values from -2 to 2
- spectral_weight: bfloat16 [4, 16, 32, 2, 64, 64], P('segment', 'space'), may hold values from -0.5 to 0.5
- proj_weight: bfloat16 [64, 128], replicated, may hold values from -0.75 to 0.75
- proj_bias: float32 [128], replicated, may hold values from -3 to 3
- out_weight: bfloat16 [128], replicated, may hold values from -0.5 to 0.5
Outputs:
- spectral_grad: float32 [8, 16, 32, 2, 64, 64], P(('groups', 'segment'), 'space'), parts along dimension 0
- point_grad: float32 [8, 64, 64], P(('groups', 'segment')), parts along dimension 0
There are 2 independent parts, one for each index of `groups`. A program takes and returns all parts, laid end to end along the dimension named above; an argument that names none is the same for every part. Nothing has to cross between parts.
All inputs are finite; a program needn't handle non-finite values.
Results may differ from a plain program's by a relative error of at most 0.033.
Values may be sent and summed in bfloat16 or wider, within the bound.
A program may use at most 64 MiB of HBM per device.

v0:
```python
from functools import partial
import math

import jax
import jax.numpy as jnp
from jax import lax
from jax.sharding import PartitionSpec as P

highest = lax.Precision.HIGHEST


def as_sent(array):
    return jax.tree.map(lambda a: a.astype(jnp.bfloat16) if a.dtype == jnp.float32 else a, array)


def passed_along(block, axis, distance):
    devices = range(lax.axis_size(axis))
    route = [(i - distance, i) for i in devices if i - distance in devices]
    return lax.ppermute(block, axis, route)


def y_tables(col_count, mode_count):
    ycells = jnp.arange(col_count, dtype=jnp.int32)[:, None]
    ymodes = jnp.arange(mode_count, dtype=jnp.int32)[None, :]
    angles = (ycells * ymodes % col_count).astype(jnp.float32) * (2.0 * math.pi / col_count)
    factor = 1.0 / math.sqrt(col_count)
    forward = jnp.stack([jnp.cos(angles), -jnp.sin(angles)], axis=1) * factor
    doubled = jnp.where(ymodes == 0, 1.0, 2.0).astype(jnp.float32)
    inverse = jnp.stack([doubled * jnp.cos(angles), -doubled * jnp.sin(angles)], axis=0) * factor
    return (forward.astype(jnp.bfloat16), jnp.transpose(inverse, (0, 2, 1)).astype(jnp.bfloat16))


def x_tables(row_total, mode_count):
    kx_count = 2 * mode_count
    indices = jnp.arange(kx_count, dtype=jnp.int32)
    freq_values = jnp.where(indices < mode_count, indices, indices - kx_count)
    xcells = jnp.arange(row_total, dtype=jnp.int32)
    angles = (freq_values[:, None] * xcells[None, :] % row_total).astype(jnp.float32) * (
        2.0 * math.pi / row_total
    )
    factor = 1.0 / math.sqrt(row_total)
    cosine_part = jnp.cos(angles) * factor
    sine_part = jnp.sin(angles) * factor
    forward = jnp.stack(
        [jnp.stack([cosine_part, sine_part], -1), jnp.stack([-sine_part, cosine_part], -1)], axis=1
    )
    cosine_flip = cosine_part.T
    sine_flip = sine_part.T
    inverse = jnp.stack(
        [jnp.stack([cosine_flip, -sine_flip], -1), jnp.stack([sine_flip, cosine_flip], -1)], axis=1
    )
    return (forward, inverse)


def mode_mult(coeffs, kernel):
    real_in, imag_in = (coeffs[:, :, 0], coeffs[:, :, 1])
    real_kernel, imag_kernel = (kernel[:, :, 0], kernel[:, :, 1])
    product = partial(jnp.einsum, "mjc,mjco->mjo", precision=highest)
    real_out = product(real_in, real_kernel) - product(imag_in, imag_kernel)
    imag_out = product(real_in, imag_kernel) + product(imag_in, real_kernel)
    return jnp.stack([real_out, imag_out], axis=2)


def mode_back(coeffs, mode_grads, kernel):
    real_in, imag_in = (coeffs[:, :, 0], coeffs[:, :, 1])
    real_grad, imag_grad = (mode_grads[:, :, 0], mode_grads[:, :, 1])
    real_kernel, imag_kernel = (kernel[:, :, 0], kernel[:, :, 1])
    outer_sum = partial(jnp.einsum, "mjc,mjo->mjco", precision=highest)
    inner_sum = partial(jnp.einsum, "mjo,mjco->mjc", precision=highest)
    kernel_real = outer_sum(real_in, real_grad) + outer_sum(imag_in, imag_grad)
    kernel_imag = outer_sum(real_in, imag_grad) - outer_sum(imag_in, real_grad)
    coeff_real = inner_sum(real_grad, real_kernel) + inner_sum(imag_grad, imag_kernel)
    coeff_imag = inner_sum(imag_grad, real_kernel) - inner_sum(real_grad, imag_kernel)
    return (
        jnp.stack([kernel_real, kernel_imag], axis=2),
        jnp.stack([coeff_real, coeff_imag], axis=2),
    )


def gelu_grad(pre_act, upstream):
    _, pullback = jax.vjp(jax.nn.gelu, pre_act)
    return pullback(upstream)[0]


def store_slot(buffer, value, slot_clip, is_valid):
    previous = lax.dynamic_index_in_dim(buffer, slot_clip, 0, keepdims=False)
    return lax.dynamic_update_index_in_dim(
        buffer, jnp.where(is_valid, value, previous), slot_clip, 0
    )


def on_device(
    inputs,
    cotangent,
    lift_weight,
    lift_bias,
    point_weight,
    layer_bias,
    spectral_weight,
    proj_weight,
    proj_bias,
    out_weight,
):
    batch_count, row_count, _, col_count = inputs.shape
    segment_count = lax.axis_size("segment")
    segment_index = lax.axis_index("segment")
    space_count = lax.axis_size("space")
    owned_modes = spectral_weight.shape[1]
    kx_count = spectral_weight.shape[2]
    channels = point_weight.shape[1]
    mode_count = kx_count // 2
    y_forward, y_inverse = y_tables(col_count, mode_count)
    x_forward, x_inverse = x_tables(row_count * space_count, mode_count)
    x_forward_adj = jnp.transpose(x_forward, (2, 3, 0, 1))
    x_inverse_adj = jnp.transpose(x_inverse, (2, 3, 0, 1))
    y_forward_wide = y_forward.astype(jnp.float32)
    y_inverse_wide = y_inverse.astype(jnp.float32)
    kernel = spectral_weight[0].astype(jnp.float32)
    point_matrix = point_weight[0]
    bias_vector = layer_bias[0]
    tick_count = batch_count + segment_count - 1

    def to_owners(y_coeffs, x_table):
        exchanged = lax.all_to_all(
            y_coeffs.astype(jnp.bfloat16), "space", split_axis=1, concat_axis=0, tiled=True
        ).astype(y_coeffs.dtype)
        return jnp.einsum("jqxp,xmpc->mjqc", x_table, exchanged, precision=highest)

    def from_owners(owned, x_table):
        spread = jnp.einsum("xpjq,mjqc->xmpc", x_table, owned, precision=highest)
        return lax.all_to_all(
            as_sent(spread), "space", split_axis=0, concat_axis=1, tiled=True
        ).astype(spread.dtype)

    def lifted(pick_slot):
        sample = lax.dynamic_index_in_dim(inputs, pick_slot, 0, keepdims=False)
        mixed = jnp.einsum("xty,tc->xcy", sample, lift_weight, preferred_element_type=jnp.float32)
        return (mixed + lift_bias[None, :, None]).astype(jnp.bfloat16)

    def forward_tick(state_now, tick_now):
        incoming, pre_store, act_store, mode_store = state_now
        pick_slot = jnp.clip(tick_now, 0, batch_count - 1)
        layer_in = lax.cond(segment_index == 0, lambda: lifted(pick_slot), lambda: incoming)
        y_coeffs = jnp.einsum(
            "xcy,ypm->xmpc", layer_in, y_forward, preferred_element_type=jnp.float32
        )
        coeffs = to_owners(y_coeffs, x_forward)
        back_rows = from_owners(mode_mult(coeffs, kernel), x_inverse)
        branch = jnp.einsum("xmpc,pmy->xcy", back_rows, y_inverse_wide, precision=highest)
        pointwise = jnp.einsum(
            "xcy,co->xoy", layer_in, point_matrix, preferred_element_type=jnp.float32
        )
        pre_act = pointwise + branch + bias_vector[None, :, None]
        slot_index = tick_now - segment_index
        is_valid = (slot_index >= 0) & (slot_index < batch_count)
        slot_clip = jnp.clip(slot_index, 0, batch_count - 1)
        pre_store = store_slot(pre_store, pre_act, slot_clip, is_valid)
        act_store = store_slot(act_store, layer_in, slot_clip, is_valid)
        mode_store = store_slot(mode_store, coeffs, slot_clip, is_valid)
        layer_out = jax.nn.gelu(pre_act).astype(jnp.bfloat16)
        sent = passed_along(layer_out, "segment", 1)
        return ((sent, pre_store, act_store, mode_store), None)

    start_state = (
        jnp.zeros((row_count, channels, col_count), jnp.bfloat16),
        jnp.zeros((batch_count, row_count, channels, col_count), jnp.float32),
        jnp.zeros((batch_count, row_count, channels, col_count), jnp.bfloat16),
        jnp.zeros((batch_count, owned_modes, kx_count, 2, channels), jnp.float32),
    )
    final_state, _ = lax.scan(forward_tick, start_state, jnp.arange(tick_count, dtype=jnp.int32))
    _, pre_store, act_store, mode_store = final_state

    def top_grad(slot_clip, pre_act):
        top_act = jax.nn.gelu(pre_act).astype(jnp.bfloat16)
        hidden = jnp.einsum("xcy,ck->xky", top_act, proj_weight, preferred_element_type=jnp.float32)
        hidden = hidden + proj_bias[None, :, None]
        target = lax.dynamic_index_in_dim(cotangent, slot_clip, 0, keepdims=False)
        upstream = (
            out_weight.astype(jnp.float32)[None, :, None] * target.astype(jnp.float32)[:, None, :]
        )
        hidden_grad = gelu_grad(hidden, upstream).astype(jnp.bfloat16)
        return jnp.einsum(
            "xky,ck->xcy", hidden_grad, proj_weight, preferred_element_type=jnp.float32
        ).astype(jnp.bfloat16)

    def backward_tick(state_now, tick_now):
        incoming, point_sum, kernel_sum = state_now
        slot_index = tick_now - (segment_count - 1 - segment_index)
        is_valid = (slot_index >= 0) & (slot_index < batch_count)
        slot_clip = jnp.clip(slot_index, 0, batch_count - 1)
        pre_act = lax.dynamic_index_in_dim(pre_store, slot_clip, 0, keepdims=False)
        layer_in = lax.dynamic_index_in_dim(act_store, slot_clip, 0, keepdims=False)
        coeffs = lax.dynamic_index_in_dim(mode_store, slot_clip, 0, keepdims=False)
        grad_out = lax.cond(
            segment_index == segment_count - 1,
            lambda: top_grad(slot_clip, pre_act),
            lambda: incoming,
        )
        pre_grad = gelu_grad(pre_act, grad_out.astype(jnp.float32)).astype(jnp.bfloat16)
        point_term = jnp.einsum(
            "xcy,xoy->co", layer_in, pre_grad, preferred_element_type=jnp.float32
        )
        y_grads = jnp.einsum(
            "xoy,pmy->xmpo", pre_grad, y_inverse, preferred_element_type=jnp.float32
        )
        mode_grads = to_owners(y_grads, x_inverse_adj)
        kernel_step, coeff_step = mode_back(coeffs, mode_grads, kernel)
        back_rows = from_owners(coeff_step, x_forward_adj)
        back_branch = jnp.einsum("xmpc,ypm->xcy", back_rows, y_forward_wide, precision=highest)
        pointwise_back = jnp.einsum(
            "co,xoy->xcy", point_matrix, pre_grad, preferred_element_type=jnp.float32
        )
        grad_in = (pointwise_back + back_branch).astype(jnp.bfloat16)
        point_sum = point_sum + jnp.where(is_valid, point_term, 0.0)
        kernel_sum = kernel_sum + jnp.where(is_valid, kernel_step, 0.0)
        sent = passed_along(grad_in, "segment", -1)
        return ((sent, point_sum, kernel_sum), None)

    back_start = (
        jnp.zeros((row_count, channels, col_count), jnp.bfloat16),
        jnp.zeros((channels, channels), jnp.float32),
        jnp.zeros((owned_modes, kx_count, 2, channels, channels), jnp.float32),
    )
    back_state, _ = lax.scan(backward_tick, back_start, jnp.arange(tick_count, dtype=jnp.int32))
    _, point_sum, kernel_sum = back_state
    point_total = lax.psum(point_sum, "space")
    factor = 1.0 / math.sqrt(batch_count * row_count * space_count * col_count)
    return (kernel_sum[None], (point_total * factor)[None])


def solution(mesh):
    in_specs = (
        P("groups", "space", None, None),
        P("groups", "space", None),
        P(),
        P(),
        P("segment", None, None),
        P("segment", None),
        P("segment", "space", None, None, None, None),
        P(),
        P(),
        P(),
    )
    out_specs = (
        P(("groups", "segment"), "space", None, None, None, None),
        P(("groups", "segment"), None, None),
    )
    return jax.shard_map(
        on_device, mesh=mesh, in_specs=in_specs, out_specs=out_specs, check_vma=False
    )
```

profile of v0, /device:TPU:3, one launch (start us, length us, event | category | flops | bytes accessed | tf_op | source)
XLA Modules:
  0.0 617.1 jit_solution(17774434167392830245)
XLA Ops:
  10.8 236.3 %while.40 = (s32[]{:T(128)}, bf16[8,64,256]{2,1,0:T(8,128)(2,1)S(1)}, f32[2,8,64,256]{3,2,1,0:T(8,128)S(1)}, bf16[2,8,64,256]{3,2,1,0:T(8,128)(2,1)S(1)}, f32[2,...) while((s32[]{:T(128)}, ...), condition=%wide.region_3.4_spmd, body=%wide.region_0.3_spmd.sunk | while | flops 129974280 | bytes 43396328 | solution.py:170
  95.3 8.6 %collective-permute-done = bf16[8,64,256]{2,1,0:T(8,128)(2,1)S(1)} collective-permute-done((bf16[8,64,256]{2,1,0:T(8,128)(2,1)S(1)}, bf16[8,64,256]{2,1,0:T(8,128)(2,1)S(1)}, u32[]{:S(2)}, u32[]{:S(2)}) %collective-permute-start) | collective-permute-done | bytes 262176 | tf_op jit(solution)/shard_map/while/body/eval_jaxpr/ppermute | solution.py:19
  143.0 8.6 %collective-permute-done = bf16[8,64,256]{2,1,0:T(8,128)(2,1)S(1)} collective-permute-done((bf16[8,64,256]{2,1,0:T(8,128)(2,1)S(1)}, bf16[8,64,256]{2,1,0:T(8,128)(2,1)S(1)}, u32[]{:S(2)}, u32[]{:S(2)}) %collective-permute-start) | collective-permute-done | bytes 262176 | tf_op jit(solution)/shard_map/while/body/eval_jaxpr/ppermute | solution.py:19
  190.7 8.6 %collective-permute-done = bf16[8,64,256]{2,1,0:T(8,128)(2,1)S(1)} collective-permute-done((bf16[8,64,256]{2,1,0:T(8,128)(2,1)S(1)}, bf16[8,64,256]{2,1,0:T(8,128)(2,1)S(1)}, u32[]{:S(2)}, u32[]{:S(2)}) %collective-permute-start) | collective-permute-done | bytes 262176 | tf_op jit(solution)/shard_map/while/body/eval_jaxpr/ppermute | solution.py:19
  238.5 8.6 %collective-permute-done = bf16[8,64,256]{2,1,0:T(8,128)(2,1)S(1)} collective-permute-done((bf16[8,64,256]{2,1,0:T(8,128)(2,1)S(1)}, bf16[8,64,256]{2,1,0:T(8,128)(2,1)S(1)}, u32[]{:S(2)}, u32[]{:S(2)}) %collective-permute-start) | collective-permute-done | bytes 262176 | tf_op jit(solution)/shard_map/while/body/eval_jaxpr/ppermute | solution.py:19
  247.1 353.4 %while.41 = (s32[]{:T(128)}, bf16[8,64,256]{2,1,0:T(8,128)(2,1)S(1)}, f32[64,64]{1,0:T(8,128)}, f32[4,32,2,64,64]{4,3,2,1,0:T(8,128)}, pred[]{:T(512)}, /*index=...) while((s32[]{:T(128)}, ...), condition=%wide.region_7.8_spmd.clone, body=%wide.region_4.7_spmd.clone.sunk | while | flops 227227776 | bytes 42694932 | solution.py:224
  262.9 8.3 %fusion.282 = f32[4,32,1,64]{3,2,1,0:T(1,128)S(1)} fusion(f32[4,32,64,1]{2,3,1,0:T(1,128)S(1)} %bitcast.491, f32[4,32,2,64,64]{4,3,2,1,0:T(8,128)} %get-tuple-element.1103), kind=kOutput, calls=%fused_computation.118.clone.1 | convolution fusion | flops 6291456 | bytes 4259840 | tf_op jit(solution)/shard_map/while/body/eval_jaxpr/mjo,mjco->mjc/dot_general | solution.py:72
  271.2 8.3 %fusion.281 = f32[4,32,1,64]{3,2,1,0:T(1,128)S(1)} fusion(f32[4,32,64,1]{2,3,1,0:T(1,128)S(1)} %bitcast.492, f32[4,32,2,64,64]{4,3,2,1,0:T(8,128)} %get-tuple-element.1103), kind=kOutput, calls=%fused_computation.112.clone.1 | convolution fusion | flops 6291456 | bytes 4259840 | tf_op jit(solution)/shard_map/while/body/eval_jaxpr/mjo,mjco->mjc/dot_general | solution.py:73
  279.6 8.3 %fusion.283 = f32[4,32,1,64]{3,2,1,0:T(1,128)S(1)} fusion(f32[4,32,64,1]{2,3,1,0:T(1,128)S(1)} %bitcast.487, f32[4,32,2,64,64]{4,3,2,1,0:T(8,128)} %get-tuple-element.1103), kind=kOutput, calls=%fused_computation.114.clone.1 | convolution fusion | flops 6291456 | bytes 4259840 | tf_op jit(solution)/shard_map/while/body/eval_jaxpr/mjo,mjco->mjc/dot_general | solution.py:72
  287.9 8.3 %fusion.280 = f32[4,32,1,64]{3,2,1,0:T(1,128)S(1)} fusion(f32[4,32,64,1]{2,3,1,0:T(1,128)S(1)} %bitcast.488, f32[4,32,2,64,64]{4,3,2,1,0:T(8,128)} %get-tuple-element.1103), kind=kOutput, calls=%fused_computation.116.clone.1 | convolution fusion | flops 6291456 | bytes 4259840 | tf_op jit(solution)/shard_map/while/body/eval_jaxpr/mjo,mjco->mjc/dot_general | solution.py:73
  334.9 8.3 %fusion.282 = f32[4,32,1,64]{3,2,1,0:T(1,128)S(1)} fusion(f32[4,32,64,1]{2,3,1,0:T(1,128)S(1)} %bitcast.491, f32[4,32,2,64,64]{4,3,2,1,0:T(8,128)} %get-tuple-element.1103), kind=kOutput, calls=%fused_computation.118.clone.1 | convolution fusion | flops 6291456 | bytes 4259840 | tf_op jit(solution)/shard_map/while/body/eval_jaxpr/mjo,mjco->mjc/dot_general | solution.py:72
  343.2 8.3 %fusion.281 = f32[4,32,1,64]{3,2,1,0:T(1,128)S(1)} fusion(f32[4,32,64,1]{2,3,1,0:T(1,128)S(1)} %bitcast.492, f32[4,32,2,64,64]{4,3,2,1,0:T(8,128)} %get-tuple-element.1103), kind=kOutput, calls=%fused_computation.112.clone.1 | convolution fusion | flops 6291456 | bytes 4259840 | tf_op jit(solution)/shard_map/while/body/eval_jaxpr/mjo,mjco->mjc/dot_general | solution.py:73
  359.8 8.3 %fusion.280 = f32[4,32,1,64]{3,2,1,0:T(1,128)S(1)} fusion(f32[4,32,64,1]{2,3,1,0:T(1,128)S(1)} %bitcast.488, f32[4,32,2,64,64]{4,3,2,1,0:T(8,128)} %get-tuple-element.1103), kind=kOutput, calls=%fused_computation.116.clone.1 | convolution fusion | flops 6291456 | bytes 4259840 | tf_op jit(solution)/shard_map/while/body/eval_jaxpr/mjo,mjco->mjc/dot_general | solution.py:73
  379.3 9.4 %fusion.287 = f32[4,32,2,64,64]{4,3,2,1,0:T(8,128)} fusion(f32[4,32,1,64,64]{4,3,2,1,0:T(8,128)} %get-tuple-element.977, f32[4,32,1,64,64]{4,3,2,1,0:T(8,128)} %get-tuple-element.978, f32[4,32,2,64,64]{4,3,2,1,0:T(8,128)} %get-tuple-element.1068, pred[]{:T(512)S(6)} %compare.49, pred[]{:T(512)S(6)} %and.179), kind=kLoop, calls=%fused_computation.111.clone.1 | loop fusion | flops 4194304 | bytes 12582914 | tf_op jit(solution)/shard_map/while/body/eval_jaxpr/add | solution.py:215
  405.5 8.3 %fusion.282 = f32[4,32,1,64]{3,2,1,0:T(1,128)S(1)} fusion(f32[4,32,64,1]{2,3,1,0:T(1,128)S(1)} %bitcast.491, f32[4,32,2,64,64]{4,3,2,1,0:T(8,128)} %get-tuple-element.1103), kind=kOutput, calls=%fused_computation.118.clone.1 | convolution fusion | flops 6291456 | bytes 4259840 | tf_op jit(solution)/shard_map/while/body/eval_jaxpr/mjo,mjco->mjc/dot_general | solution.py:72
  413.8 8.3 %fusion.281 = f32[4,32,1,64]{3,2,1,0:T(1,128)S(1)} fusion(f32[4,32,64,1]{2,3,1,0:T(1,128)S(1)} %bitcast.492, f32[4,32,2,64,64]{4,3,2,1,0:T(8,128)} %get-tuple-element.1103), kind=kOutput, calls=%fused_computation.112.clone.1 | convolution fusion | flops 6291456 | bytes 4259840 | tf_op jit(solution)/shard_map/while/body/eval_jaxpr/mjo,mjco->mjc/dot_general | solution.py:73
  422.1 8.3 %fusion.283 = f32[4,32,1,64]{3,2,1,0:T(1,128)S(1)} fusion(f32[4,32,64,1]{2,3,1,0:T(1,128)S(1)} %bitcast.487, f32[4,32,2,64,64]{4,3,2,1,0:T(8,128)} %get-tuple-element.1103), kind=kOutput, calls=%fused_computation.114.clone.1 | convolution fusion | flops 6291456 | bytes 4259840 | tf_op jit(solution)/shard_map/while/body/eval_jaxpr/mjo,mjco->mjc/dot_general | solution.py:72
  430.4 8.3 %fusion.280 = f32[4,32,1,64]{3,2,1,0:T(1,128)S(1)} fusion(f32[4,32,64,1]{2,3,1,0:T(1,128)S(1)} %bitcast.488, f32[4,32,2,64,64]{4,3,2,1,0:T(8,128)} %get-tuple-element.1103), kind=kOutput, calls=%fused_computation.116.clone.1 | convolution fusion | flops 6291456 | bytes 4259840 | tf_op jit(solution)/shard_map/while/body/eval_jaxpr/mjo,mjco->mjc/dot_general | solution.py:73
  449.9 9.4 %fusion.287 = f32[4,32,2,64,64]{4,3,2,1,0:T(8,128)} fusion(f32[4,32,1,64,64]{4,3,2,1,0:T(8,128)} %get-tuple-element.977, f32[4,32,1,64,64]{4,3,2,1,0:T(8,128)} %get-tuple-element.978, f32[4,32,2,64,64]{4,3,2,1,0:T(8,128)} %get-tuple-element.1068, pred[]{:T(512)S(6)} %compare.49, pred[]{:T(512)S(6)} %and.179), kind=kLoop, calls=%fused_computation.111.clone.1 | loop fusion | flops 4194304 | bytes 12582914 | tf_op jit(solution)/shard_map/while/body/eval_jaxpr/add | solution.py:215
  476.1 8.3 %fusion.282 = f32[4,32,1,64]{3,2,1,0:T(1,128)S(1)} fusion(f32[4,32,64,1]{2,3,1,0:T(1,128)S(1)} %bitcast.491, f32[4,32,2,64,64]{4,3,2,1,0:T(8,128)} %get-tuple-element.1103), kind=kOutput, calls=%fused_computation.118.clone.1 | convolution fusion | flops 6291456 | bytes 4259840 | tf_op jit(solution)/shard_map/while/body/eval_jaxpr/mjo,mjco->mjc/dot_general | solution.py:72
  520.5 9.4 %fusion.287 = f32[4,32,2,64,64]{4,3,2,1,0:T(8,128)} fusion(f32[4,32,1,64,64]{4,3,2,1,0:T(8,128)} %get-tuple-element.977, f32[4,32,1,64,64]{4,3,2,1,0:T(8,128)} %get-tuple-element.978, f32[4,32,2,64,64]{4,3,2,1,0:T(8,128)} %get-tuple-element.1068, pred[]{:T(512)S(6)} %compare.49, pred[]{:T(512)S(6)} %and.179), kind=kLoop, calls=%fused_computation.111.clone.1 | loop fusion | flops 4194304 | bytes 12582914 | tf_op jit(solution)/shard_map/while/body/eval_jaxpr/add | solution.py:215
  546.7 8.3 %fusion.282 = f32[4,32,1,64]{3,2,1,0:T(1,128)S(1)} fusion(f32[4,32,64,1]{2,3,1,0:T(1,128)S(1)} %bitcast.491, f32[4,32,2,64,64]{4,3,2,1,0:T(8,128)} %get-tuple-element.1103), kind=kOutput, calls=%fused_computation.118.clone.1 | convolution fusion | flops 6291456 | bytes 4259840 | tf_op jit(solution)/shard_map/while/body/eval_jaxpr/mjo,mjco->mjc/dot_general | solution.py:72
  591.1 9.4 %fusion.287 = f32[4,32,2,64,64]{4,3,2,1,0:T(8,128)} fusion(f32[4,32,1,64,64]{4,3,2,1,0:T(8,128)} %get-tuple-element.977, f32[4,32,1,64,64]{4,3,2,1,0:T(8,128)} %get-tuple-element.978, f32[4,32,2,64,64]{4,3,2,1,0:T(8,128)} %get-tuple-element.1068, pred[]{:T(512)S(6)} %compare.49, pred[]{:T(512)S(6)} %and.179), kind=kLoop, calls=%fused_computation.111.clone.1 | loop fusion | flops 4194304 | bytes 12582914 | tf_op jit(solution)/shard_map/while/body/eval_jaxpr/add | solution.py:215
  600.5 16.0 %psum.7 = f32[64,64]{1,0:T(8,128)S(1)} all-reduce(f32[64,64]{1,0:T(8,128)} %get-tuple-element.457), channel_id=1, replica_groups=mesh['groups'=2,'segment'=4,'space'=4] {'space'}, use_global_device_ids=true, to_apply=%region_8.9 | all-reduce | flops 4096 | bytes 32768 | tf_op jit(solution)/shard_map/psum | solution.py:226
  (371 shorter events, 428.8 us)
Async XLA Ops:
  12.5 9.1 %all-to-all-start = ((bf16[4,2,2048]{2,1,0:T(2,128)(2,1)}), bf16[4,2,2048]{2,1,0:T(2,128)(2,1)S(1)}, u32[]{:S(2)}, u32[]{:S(2)}) async-start(bf16[4,2,2048]{2,1,0:T(2,128)(2,1)} %reshape.533), calls=%async_computation | async-start | bytes 65536 | tf_op jit(solution)/shard_map/while/body/eval_jaxpr/all_to_all | solution.py:124
  41.3 7.7 %all-to-all-start.1 = ((bf16[4,2,2048]{2,1,0:T(2,128)(2,1)}), bf16[4,2,2048]{2,1,0:T(2,128)(2,1)S(1)}, u32[]{:S(2)}, u32[]{:S(2)}) async-start(bf16[4,2,2048]{2,1,0:T(2,128)(2,1)} %reshape.535), calls=%async_computation.1 | async-start | bytes 65536 | tf_op jit(solution)/shard_map/while/body/eval_jaxpr/all_to_all | solution.py:131
  57.8 7.7 %all-to-all-start = ((bf16[4,2,2048]{2,1,0:T(2,128)(2,1)}), bf16[4,2,2048]{2,1,0:T(2,128)(2,1)S(1)}, u32[]{:S(2)}, u32[]{:S(2)}) async-start(bf16[4,2,2048]{2,1,0:T(2,128)(2,1)} %reshape.533), calls=%async_computation | async-start | bytes 65536 | tf_op jit(solution)/shard_map/while/body/eval_jaxpr/all_to_all | solution.py:124
  85.2 7.7 %all-to-all-start.1 = ((bf16[4,2,2048]{2,1,0:T(2,128)(2,1)}), bf16[4,2,2048]{2,1,0:T(2,128)(2,1)S(1)}, u32[]{:S(2)}, u32[]{:S(2)}) async-start(bf16[4,2,2048]{2,1,0:T(2,128)(2,1)} %reshape.535), calls=%async_computation.1 | async-start | bytes 65536 | tf_op jit(solution)/shard_map/while/body/eval_jaxpr/all_to_all | solution.py:131
  93.9 10.0 %collective-permute-start = (bf16[8,64,256]{2,1,0:T(8,128)(2,1)S(1)}, bf16[8,64,256]{2,1,0:T(8,128)(2,1)S(1)}, u32[]{:S(2)}, u32[]{:S(2)}) collective-permute-start(bf16[8,64,256]{2,1,0:T(8,128)(2,1)S(1)} %get-tuple-element.946), channel_id=1, source_target_pairs={{0,4},{4,8},{8,12},{1,5},{5,9},{9,13},{2,6},{6,10},{10,14},{3,7},{... | collective-permute-start | bytes 786440 | tf_op jit(solution)/shard_map/while/body/eval_jaxpr/ppermute | solution.py:19
  141.6 10.0 %collective-permute-start = (bf16[8,64,256]{2,1,0:T(8,128)(2,1)S(1)}, bf16[8,64,256]{2,1,0:T(8,128)(2,1)S(1)}, u32[]{:S(2)}, u32[]{:S(2)}) collective-permute-start(bf16[8,64,256]{2,1,0:T(8,128)(2,1)S(1)} %get-tuple-element.946), channel_id=1, source_target_pairs={{0,4},{4,8},{8,12},{1,5},{5,9},{9,13},{2,6},{6,10},{10,14},{3,7},{... | collective-permute-start | bytes 786440 | tf_op jit(solution)/shard_map/while/body/eval_jaxpr/ppermute | solution.py:19
  153.2 7.7 %all-to-all-start = ((bf16[4,2,2048]{2,1,0:T(2,128)(2,1)}), bf16[4,2,2048]{2,1,0:T(2,128)(2,1)S(1)}, u32[]{:S(2)}, u32[]{:S(2)}) async-start(bf16[4,2,2048]{2,1,0:T(2,128)(2,1)} %reshape.533), calls=%async_computation | async-start | bytes 65536 | tf_op jit(solution)/shard_map/while/body/eval_jaxpr/all_to_all | solution.py:124
  189.4 10.0 %collective-permute-start = (bf16[8,64,256]{2,1,0:T(8,128)(2,1)S(1)}, bf16[8,64,256]{2,1,0:T(8,128)(2,1)S(1)}, u32[]{:S(2)}, u32[]{:S(2)}) collective-permute-start(bf16[8,64,256]{2,1,0:T(8,128)(2,1)S(1)} %get-tuple-element.946), channel_id=1, source_target_pairs={{0,4},{4,8},{8,12},{1,5},{5,9},{9,13},{2,6},{6,10},{10,14},{3,7},{... | collective-permute-start | bytes 786440 | tf_op jit(solution)/shard_map/while/body/eval_jaxpr/ppermute | solution.py:19
  228.4 7.7 %all-to-all-start.1 = ((bf16[4,2,2048]{2,1,0:T(2,128)(2,1)}), bf16[4,2,2048]{2,1,0:T(2,128)(2,1)S(1)}, u32[]{:S(2)}, u32[]{:S(2)}) async-start(bf16[4,2,2048]{2,1,0:T(2,128)(2,1)} %reshape.535), calls=%async_computation.1 | async-start | bytes 65536 | tf_op jit(solution)/shard_map/while/body/eval_jaxpr/all_to_all | solution.py:131
  237.1 10.0 %collective-permute-start = (bf16[8,64,256]{2,1,0:T(8,128)(2,1)S(1)}, bf16[8,64,256]{2,1,0:T(8,128)(2,1)S(1)}, u32[]{:S(2)}, u32[]{:S(2)}) collective-permute-start(bf16[8,64,256]{2,1,0:T(8,128)(2,1)S(1)} %get-tuple-element.946), channel_id=1, source_target_pairs={{0,4},{4,8},{8,12},{1,5},{5,9},{9,13},{2,6},{6,10},{10,14},{3,7},{... | collective-permute-start | bytes 786440 | tf_op jit(solution)/shard_map/while/body/eval_jaxpr/ppermute | solution.py:19
  297.3 7.9 %all-to-all-start.3 = ((bf16[4,2,2048]{2,1,0:T(2,128)(2,1)}), bf16[4,2,2048]{2,1,0:T(2,128)(2,1)S(1)}, u32[]{:S(2)}, u32[]{:S(2)}) async-start(bf16[4,2,2048]{2,1,0:T(2,128)(2,1)} %reshape.539), calls=%async_computation.3 | async-start | bytes 65536 | tf_op jit(solution)/shard_map/while/body/eval_jaxpr/all_to_all | solution.py:131
  306.0 12.8 %collective-permute-start.1 = (bf16[8,64,256]{2,1,0:T(8,128)(2,1)S(1)}, bf16[8,64,256]{2,1,0:T(8,128)(2,1)S(1)}, u32[]{:S(2)}, u32[]{:S(2)}) collective-permute-start(bf16[8,64,256]{2,1,0:T(8,128)(2,1)S(1)} %fusion.285), channel_id=1, source_target_pairs={{4,0},{8,4},{12,8},{5,1},{9,5},{13,9},{6,2},{10,6},{14,10},{7,3},{... | collective-permute-start | bytes 786440 | tf_op jit(solution)/shard_map/while/body/eval_jaxpr/ppermute | solution.py:19
  326.2 8.3 %all-to-all-start.2 = ((bf16[4,2,2048]{2,1,0:T(2,128)(2,1)}), bf16[4,2,2048]{2,1,0:T(2,128)(2,1)S(1)}, u32[]{:S(2)}, u32[]{:S(2)}) async-start(bf16[4,2,2048]{2,1,0:T(2,128)(2,1)} %reshape.537), calls=%async_computation.2 | async-start | bytes 65536 | tf_op jit(solution)/shard_map/while/body/eval_jaxpr/all_to_all | solution.py:124
  369.3 7.9 %all-to-all-start.3 = ((bf16[4,2,2048]{2,1,0:T(2,128)(2,1)}), bf16[4,2,2048]{2,1,0:T(2,128)(2,1)S(1)}, u32[]{:S(2)}, u32[]{:S(2)}) async-start(bf16[4,2,2048]{2,1,0:T(2,128)(2,1)} %reshape.539), calls=%async_computation.3 | async-start | bytes 65536 | tf_op jit(solution)/shard_map/while/body/eval_jaxpr/all_to_all | solution.py:131
  378.0 10.7 %collective-permute-start.1 = (bf16[8,64,256]{2,1,0:T(8,128)(2,1)S(1)}, bf16[8,64,256]{2,1,0:T(8,128)(2,1)S(1)}, u32[]{:S(2)}, u32[]{:S(2)}) collective-permute-start(bf16[8,64,256]{2,1,0:T(8,128)(2,1)S(1)} %fusion.285), channel_id=1, source_target_pairs={{4,0},{8,4},{12,8},{5,1},{9,5},{13,9},{6,2},{10,6},{14,10},{7,3},{... | collective-permute-start | bytes 786440 | tf_op jit(solution)/shard_map/while/body/eval_jaxpr/ppermute | solution.py:19
  396.1 9.0 %all-to-all-start.2 = ((bf16[4,2,2048]{2,1,0:T(2,128)(2,1)}), bf16[4,2,2048]{2,1,0:T(2,128)(2,1)S(1)}, u32[]{:S(2)}, u32[]{:S(2)}) async-start(bf16[4,2,2048]{2,1,0:T(2,128)(2,1)} %reshape.537), calls=%async_computation.2 | async-start | bytes 65536 | tf_op jit(solution)/shard_map/while/body/eval_jaxpr/all_to_all | solution.py:124
  439.9 7.9 %all-to-all-start.3 = ((bf16[4,2,2048]{2,1,0:T(2,128)(2,1)}), bf16[4,2,2048]{2,1,0:T(2,128)(2,1)S(1)}, u32[]{:S(2)}, u32[]{:S(2)}) async-start(bf16[4,2,2048]{2,1,0:T(2,128)(2,1)} %reshape.539), calls=%async_computation.3 | async-start | bytes 65536 | tf_op jit(solution)/shard_map/while/body/eval_jaxpr/all_to_all | solution.py:131
  448.6 10.7 %collective-permute-start.1 = (bf16[8,64,256]{2,1,0:T(8,128)(2,1)S(1)}, bf16[8,64,256]{2,1,0:T(8,128)(2,1)S(1)}, u32[]{:S(2)}, u32[]{:S(2)}) collective-permute-start(bf16[8,64,256]{2,1,0:T(8,128)(2,1)S(1)} %fusion.285), channel_id=1, source_target_pairs={{4,0},{8,4},{12,8},{5,1},{9,5},{13,9},{6,2},{10,6},{14,10},{7,3},{... | collective-permute-start | bytes 786440 | tf_op jit(solution)/shard_map/while/body/eval_jaxpr/ppermute | solution.py:19
  466.7 9.0 %all-to-all-start.2 = ((bf16[4,2,2048]{2,1,0:T(2,128)(2,1)}), bf16[4,2,2048]{2,1,0:T(2,128)(2,1)S(1)}, u32[]{:S(2)}, u32[]{:S(2)}) async-start(bf16[4,2,2048]{2,1,0:T(2,128)(2,1)} %reshape.537), calls=%async_computation.2 | async-start | bytes 65536 | tf_op jit(solution)/shard_map/while/body/eval_jaxpr/all_to_all | solution.py:124
  510.5 7.9 %all-to-all-start.3 = ((bf16[4,2,2048]{2,1,0:T(2,128)(2,1)}), bf16[4,2,2048]{2,1,0:T(2,128)(2,1)S(1)}, u32[]{:S(2)}, u32[]{:S(2)}) async-start(bf16[4,2,2048]{2,1,0:T(2,128)(2,1)} %reshape.539), calls=%async_computation.3 | async-start | bytes 65536 | tf_op jit(solution)/shard_map/while/body/eval_jaxpr/all_to_all | solution.py:131
  519.2 10.7 %collective-permute-start.1 = (bf16[8,64,256]{2,1,0:T(8,128)(2,1)S(1)}, bf16[8,64,256]{2,1,0:T(8,128)(2,1)S(1)}, u32[]{:S(2)}, u32[]{:S(2)}) collective-permute-start(bf16[8,64,256]{2,1,0:T(8,128)(2,1)S(1)} %fusion.285), channel_id=1, source_target_pairs={{4,0},{8,4},{12,8},{5,1},{9,5},{13,9},{6,2},{10,6},{14,10},{7,3},{... | collective-permute-start | bytes 786440 | tf_op jit(solution)/shard_map/while/body/eval_jaxpr/ppermute | solution.py:19
  537.3 9.0 %all-to-all-start.2 = ((bf16[4,2,2048]{2,1,0:T(2,128)(2,1)}), bf16[4,2,2048]{2,1,0:T(2,128)(2,1)S(1)}, u32[]{:S(2)}, u32[]{:S(2)}) async-start(bf16[4,2,2048]{2,1,0:T(2,128)(2,1)} %reshape.537), calls=%async_computation.2 | async-start | bytes 65536 | tf_op jit(solution)/shard_map/while/body/eval_jaxpr/all_to_all | solution.py:124
  581.1 7.9 %all-to-all-start.3 = ((bf16[4,2,2048]{2,1,0:T(2,128)(2,1)}), bf16[4,2,2048]{2,1,0:T(2,128)(2,1)S(1)}, u32[]{:S(2)}, u32[]{:S(2)}) async-start(bf16[4,2,2048]{2,1,0:T(2,128)(2,1)} %reshape.539), calls=%async_computation.3 | async-start | bytes 65536 | tf_op jit(solution)/shard_map/while/body/eval_jaxpr/all_to_all | solution.py:131
  589.8 10.7 %collective-permute-start.1 = (bf16[8,64,256]{2,1,0:T(8,128)(2,1)S(1)}, bf16[8,64,256]{2,1,0:T(8,128)(2,1)S(1)}, u32[]{:S(2)}, u32[]{:S(2)}) collective-permute-start(bf16[8,64,256]{2,1,0:T(8,128)(2,1)S(1)} %fusion.285), channel_id=1, source_target_pairs={{4,0},{8,4},{12,8},{5,1},{9,5},{13,9},{6,2},{10,6},{14,10},{7,3},{... | collective-permute-start | bytes 786440 | tf_op jit(solution)/shard_map/while/body/eval_jaxpr/ppermute | solution.py:19
  (21 other events, 386.5 us)
where the time goes:
time: 621 us; the launch traced here: 617 us
  matrix products  293 us (47%)
  waiting for transfers between devices  95 us (15%)
  starting transfers between devices  87.9 us (14%)
  other arithmetic  86.2 us (14%)
  local copies, waits for them, and re-layouts  30.1 us (5%)
  blocking collectives  16 us (3%)
  loops' own time  8.3 us (1%)
    dot_general x10, matrix products, mode_mult(): real_out = product(real_in, real_kernel) - product(imag_in, imag_kernel)  45.7 us
    dot_general x10, matrix products, mode_mult(): imag_out = product(real_in, imag_kernel) + product(imag_in, real_kernel)  44.9 us
    add x5, other arithmetic, backward_tick(): kernel_sum = kernel_sum + jnp.where(is_valid, kernel_step, 0.0)  44.7 us
    dot_general x5, matrix products, mode_back(): inner_sum(real_grad, real_kernel) + inner_sum(imag_grad, imag_kernel)  41.6 us
    dot_general x5, matrix products, mode_back(): inner_sum(real_grad, imag_kernel)  41.6 us
    dot_general x5, matrix products, mode_back(): inner_sum(imag_grad, real_kernel) - inner_sum(real_grad, imag_kernel)  41.6 us
    dot_general x5, matrix products, mode_back(): inner_sum(imag_grad, imag_kernel)  41.6 us
    ppermute x10, waiting for transfers between devices, passed_along(): return lax.ppermute(block, axis, route)  39.3 us
  transfers between devices with their start and end apart: 30, of which 20 were waited for; matrix products, arithmetic and copies ran while one was open for 12% of the time, Pallas kernels for 0%

commit v1 on v0

v1 whole, which is shorter than its diff:
```python
import functools
import math

import jax
import jax.numpy as jnp
import ml_dtypes
import numpy as np
from jax import lax
from jax.experimental import pallas as pl
from jax.experimental.pallas import tpu as pltpu
from jax.sharding import PartitionSpec as P

MESH = pl.DeviceIdType.MESH
F32 = jnp.float32
BF16 = jnp.bfloat16
VMEM_BYTES = 48 * 1024 * 1024


def dot(a, b, dims=((1,), (0,))):
    return lax.dot_general(a, b, (dims, ((), ())), preferred_element_type=F32)


def each(count, body):
    def step(i, carry):
        body(i)
        return carry

    lax.fori_loop(0, count, step, 0, unroll=count <= 64)


class Sizes:
    def __init__(self, batch, rows, cols, segments, spaces, owned, kx, channels):
        self.MB, self.rows, self.NY = batch, rows, cols
        self.L, self.S, self.own, self.J, self.C = segments, spaces, owned, kx, channels
        self.U = batch * rows // segments
        assert self.U * segments == batch * rows
        self.ML = 2 if owned % 2 == 0 and 2 * channels <= 128 else 1
        self.H = owned // self.ML
        self.RP = -(-self.U * self.H * 2 // 16) * 16
        self.LN = self.ML * channels
        self.RG = -(-self.ML * batch * 2 // 8) * 8
        self.N = segments * spaces
        self.K = self.N * self.RP
        self.R = self.H * kx * self.RG
        self.Y = self.U * cols


def make_tables(z):
    modes = z.own * z.S
    y = np.arange(z.NY)[:, None]
    m = np.arange(modes)[None, :]
    t = 2 * math.pi * ((y * m) % z.NY) / z.NY
    fy = np.stack([np.cos(t), -np.sin(t)], 1) / math.sqrt(z.NY)
    iy = fy * np.where(m == 0, 1.0, 2.0)[:, None, :]
    nx = z.rows * z.S
    f = np.arange(z.J)
    f = np.where(f < z.J // 2, f, f - z.J)
    u = 2 * math.pi * ((f[:, None] * np.arange(nx)[None, :]) % nx) / nx
    c, s = np.cos(u) / math.sqrt(nx), np.sin(u) / math.sqrt(nx)
    fx = np.stack([np.stack([c, s], -1), np.stack([-s, c], -1)], 1)
    ix = np.stack([np.stack([c.T, -s.T], -1), np.stack([s.T, c.T], -1)], 1)

    ytab = []
    for table in (fy, iy):
        out = np.zeros((z.ML, z.S, z.RP, z.U, z.NY))
        for ml in range(z.ML):
            for sp in range(z.S):
                for un in range(z.U):
                    for h in range(z.H):
                        for p in range(2):
                            mode = sp * z.own + h * z.ML + ml
                            out[ml, sp, (un * z.H + h) * 2 + p, un] = table[:, p, mode]
        ytab.append(out.reshape(z.ML * z.S * z.RP, z.Y))

    x1 = np.zeros((z.H, z.J, z.RG, z.N, z.RP))
    x2, xg = np.zeros_like(x1), np.zeros_like(x1)
    for g in range(z.L):
        for sp in range(z.S):
            for un in range(z.U):
                b, xl = divmod(g * z.U + un, z.rows)
                x = sp * z.rows + xl
                for h in range(z.H):
                    for p in range(2):
                        col = (un * z.H + h) * 2 + p
                        for ml in range(z.ML):
                            r = (ml * z.MB + b) * 2
                            at = g * z.S + sp
                            for q in range(2):
                                x1[h, :, r + q, at, col] = fx[:, q, x, p]
                                xg[h, :, r + q, at, col] = ix[x, p, :, q]
                            x2[h, :, r, at, col] = -fx[:, 1, x, p]
                            x2[h, :, r + 1, at, col] = fx[:, 0, x, p]
    xs = [a.reshape(z.R, z.K) for a in (x1, x2, xg)]
    tables = ytab + xs + [a.T for a in xs]
    return [np.ascontiguousarray(a).astype(ml_dtypes.bfloat16) for a in tables]


def gelu_parts(v):
    k = math.sqrt(2.0 / math.pi)
    v2 = v * v
    t = jnp.tanh(v * (k + (k * 0.044715) * v2))
    half = 0.5 + 0.5 * t
    return half, v2, t


def gelu_slope(v):
    k = math.sqrt(2.0 / math.pi)
    half, v2, t = gelu_parts(v)
    return half + (0.5 * v) * (1.0 - t * t) * (k + (3.0 * k * 0.044715) * v2)


def main_kernel(
    z, inputs, cotangent, lift_wt, lift_b, pack_own, weights, proj_w, proj_wt, proj_b, out_w,
    yf, yi, x1, x2, xg, x1t, x2t, xgt,
    zz_out, ll_out, pg_out,
    acts, slopes, pregrad, grad, pack, msg, recv, omsg, back, modes, spread, pgs, pgr,
    to_send, to_recv, back_send, back_recv, pg_send, pg_recv, gat_send, gat_recv,
):
    C, LN, Q = z.C, z.LN, z.MB * 2
    seg, sp = lax.axis_index("segment"), lax.axis_index("space")
    me = seg * z.S + sp
    barrier = pltpu.get_barrier_semaphore()

    def device(g, s):
        return {"segment": g, "space": s}

    def greet(i):
        @pl.when(i != me)
        def _():
            pl.semaphore_signal(
                barrier, inc=1, device_id=device(i // z.S, i % z.S), device_id_type=MESH
            )

    each(z.N, greet)

    def remote(src, dst, send, receive, g, s):
        return pltpu.make_async_remote_copy(
            src_ref=src, dst_ref=dst, send_sem=send, recv_sem=receive,
            device_id=device(g, s), device_id_type=MESH,
        )

    def to_copy(layer, s):
        return remote(msg.at[s], recv.at[me], to_send.at[s], to_recv.at[me], layer, s)

    def from_copy(src):
        return remote(
            msg.at[0], recv.at[src], to_send.at[0], to_recv.at[src], src // z.S, src % z.S
        )

    def back_copy(i):
        return remote(
            omsg.at[i], back.at[sp], back_send.at[i], back_recv.at[sp], i // z.S, i % z.S
        )

    def back_from(layer, s):
        return remote(omsg.at[0], back.at[s], back_send.at[0], back_recv.at[s], layer, s)

    def pg_copy(layer, s):
        return remote(pgs.at[layer], pgr.at[me], pg_send.at[s], pg_recv.at[me], layer, s)

    def pg_from(src):
        return remote(
            pgs.at[0], pgr.at[src], pg_send.at[0], pg_recv.at[src], src // z.S, src % z.S
        )

    def pack_copy(g):
        return remote(pack_own, pack.at[seg], gat_send.at[g], gat_recv.at[seg], g, sp)

    def pack_from(g):
        return remote(pack_own, pack.at[g], gat_send.at[g], gat_recv.at[g], g, sp)

    def other(g, s, act):
        pl.when(jnp.logical_not((seg == g) & (sp == s)))(act)

    def send_rows(layer, table, values, wait_layer):
        co = dot(table[...], values, ((1,), (1,)))
        part = z.S * z.RP
        wide = jnp.concatenate([co[i * part : (i + 1) * part] for i in range(z.ML)], axis=1)
        if wait_layer is not None:
            each(z.S, lambda s: other(wait_layer, s, lambda: to_copy(wait_layer, s).wait_send()))
        msg[...] = wide.astype(BF16).reshape(z.S, z.RP, LN)
        each(z.S, lambda s: other(layer, s, lambda: to_copy(layer, s).start()))

        @pl.when(seg == layer)
        def _():
            recv[me] = msg[sp]

    def received():
        each(z.N, lambda i: pl.when(i != me)(lambda: from_copy(i).wait_recv()))
        return recv[...].reshape(z.K, LN)

    def answer(rows):
        omsg[...] = rows.astype(BF16).reshape(z.N, z.RP, LN)
        each(z.N, lambda i: pl.when(i != me)(lambda: back_copy(i).start()))
        back[sp] = omsg[me]

    def answer_sent():
        each(z.N, lambda i: pl.when(i != me)(lambda: back_copy(i).wait_send()))

    def answered(layer):
        each(z.S, lambda s: other(layer, s, lambda: back_from(layer, s).wait_recv()))
        rows = back[...].reshape(z.S * z.RP, LN)
        return jnp.concatenate([rows[:, i * C : (i + 1) * C] for i in range(z.ML)], axis=0)

    def own_part(value):
        row = lax.broadcasted_iota(jnp.int32, value.shape, 0) % z.RG // Q
        lane = lax.broadcasted_iota(jnp.int32, value.shape, 1) // C
        return jnp.where(row == lane, value, 0.0)

    def kernel_of(i):
        h, j = i // z.J, i % z.J
        return jnp.concatenate(
            [weights[h * z.ML + ml, j, q] for q in range(2) for ml in range(z.ML)], axis=0
        )

    def group(i):
        start = i * z.RG
        return pl.ds(start if isinstance(start, int) else pl.multiple_of(start, z.RG), z.RG)

    tail = lax.broadcasted_iota(jnp.int32, (128 - C, z.Y), 0)
    tail = jnp.where(tail < 2, 1.0, 0.0).astype(BF16)
    for layer in range(z.L):
        acts[layer, C:128, :] = tail
    for u in range(z.U):
        value = dot(lift_wt[...], inputs[seg * z.U + u]) + lift_b[...]
        acts[0, 0:C, u * z.NY : (u + 1) * z.NY] = value.astype(BF16)

    pl.semaphore_wait(barrier, z.N - 1)
    send_rows(0, yf, acts[0, 0:C, :], None)
    each(z.L, lambda g: pl.when(g != seg)(lambda: pack_copy(g).start()))
    pack[seg] = pack_own[...]
    each(z.L, lambda g: pl.when(g != seg)(lambda: pack_from(g).wait_recv()))

    def forward(layer, carry):
        @pl.when(seg == layer)
        def _():
            got = received()
            zz_out[:, 0:LN] = own_part(dot(x1[...], got))
            zz_out[:, LN : 2 * LN] = own_part(dot(x2[...], got))

            def mult(i):
                modes[group(i), :] = dot(zz_out[group(i), :].astype(BF16), kernel_of(i))

            each(z.H * z.J, mult)
            product = modes[...]
            product = own_part(jnp.concatenate([product] * z.ML, axis=1))
            answer(dot(xgt[...], product.astype(BF16)))

        local = dot(pack[layer, 0], acts[layer])
        pre = local + dot(answered(layer), yi[...], ((0,), (0,)))
        half, _, _ = gelu_parts(pre)
        acts[layer + 1, 0:C, :] = (pre * half).astype(BF16)

        @pl.when(layer < z.L - 1)
        def _():
            send_rows(layer + 1, yf, acts[layer + 1, 0:C, :], layer)

        slopes[layer] = gelu_slope(pre)
        return carry

    lax.fori_loop(0, z.L, forward, 0)
    answer_sent()

    hidden = dot(proj_wt[...], acts[z.L, 0:C, :]) + proj_b[...]
    target = jnp.concatenate([cotangent[seg * z.U + u] for u in range(z.U)], axis=1)
    hidden_grad = (gelu_slope(hidden) * out_w[...] * target).astype(BF16)
    grad[...] = dot(proj_w[...], hidden_grad).astype(BF16)

    def backward(step, carry):
        layer = z.L - 1 - step
        pregrad[...] = (grad[...].astype(F32) * slopes[layer]).astype(BF16)
        send_rows(layer, yi, pregrad[...], jnp.minimum(layer + 1, z.L - 1))

        @pl.when(step > 0)
        def _():
            each(z.S, lambda s: other(layer + 1, s, lambda: pg_copy(layer + 1, s).wait_send()))

        pgs[layer] = dot(acts[layer, 0:C, :], pregrad[...], ((1,), (1,))).astype(BF16)
        each(z.S, lambda s: other(layer, s, lambda: pg_copy(layer, s).start()))

        @pl.when(seg == layer)
        def _():
            pgr[me] = pgs[layer]
            got = dot(xg[...], received())
            if z.ML > 1:
                row = lax.broadcasted_iota(jnp.int32, (z.R, C), 0) % z.RG // Q
                got = jnp.where(row == 0, got[:, 0:C], got[:, C : 2 * C])
            ll_out[...] = got

            @pl.when(layer > 0)
            def _():
                def mult(i):
                    spread[group(i), :] = dot(
                        ll_out[group(i), :].astype(BF16), kernel_of(i), ((1,), (1,))
                    )

                each(z.H * z.J, mult)
                first = own_part(spread[:, 0:LN]).astype(BF16)
                second = own_part(spread[:, LN : 2 * LN]).astype(BF16)
                answer(dot(x1t[...], first) + dot(x2t[...], second))

        @pl.when(layer > 0)
        def _():
            local = dot(pack[layer, 1][:, 0:C], pregrad[...])
            grad[...] = (local + dot(answered(layer), yf[...], ((0,), (0,)))).astype(BF16)

        return carry

    lax.fori_loop(0, z.L, backward, 0)

    each(z.N, lambda i: pl.when(i != me)(lambda: pg_from(i).wait_recv()))
    total = pgr[0].astype(F32)
    for i in range(1, z.N):
        total = total + pgr[i].astype(F32)
    pg_out[...] = total * (1.0 / math.sqrt(z.MB * z.rows * z.S * z.NY))

    each(z.S, lambda s: other(0, s, lambda: pg_copy(0, s).wait_send()))
    each(z.S, lambda s: other(0, s, lambda: to_copy(0, s).wait_send()))
    pl.when(seg > 0)(answer_sent)
    each(z.L, lambda g: pl.when(g != seg)(lambda: pack_copy(g).wait_send()))


def outer_kernel(z, count, zz, ll, out):
    turned = zz[...].T.astype(BF16)
    grads = ll[...]
    row = lax.broadcasted_iota(jnp.int32, grads.shape, 0) // z.RG
    for jj in range(count):
        part = jnp.where(row == jj, grads, 0.0).astype(BF16)
        value = dot(turned, part)
        for q in range(2):
            for ml in range(z.ML):
                at = (q * z.ML + ml) * z.C
                out[ml, jj, q] = value[at : at + z.C]


def on_device(
    inputs, cotangent, lift_weight, lift_bias, point_weight, layer_bias, spectral_weight,
    proj_weight, proj_bias, out_weight,
):
    batch, rows, steps, cols = inputs.shape
    _, owned, kx, _, C, _ = spectral_weight.shape
    z = Sizes(batch, rows, cols, lax.axis_size("segment"), lax.axis_size("space"), owned, kx, C)
    hid = proj_weight.shape[1]
    tables = [jnp.asarray(t) for t in make_tables(z)]

    w = point_weight[0]
    bias = layer_bias[0]
    high = bias.astype(BF16)
    low = (bias - high.astype(F32)).astype(BF16)
    gap = jnp.zeros((C, 128 - C - 2), BF16)
    pack = jnp.stack(
        [
            jnp.concatenate([w.T, high[:, None], low[:, None], gap], axis=1),
            jnp.concatenate([w, jnp.zeros((C, 128 - C), BF16)], axis=1),
        ]
    )
    args = [
        inputs.reshape(batch * rows, steps, cols),
        cotangent.astype(F32).reshape(batch * rows, 1, cols),
        lift_weight.T,
        lift_bias[:, None],
        pack,
        spectral_weight[0],
        proj_weight,
        proj_weight.T,
        proj_bias[:, None],
        out_weight.astype(F32)[:, None],
    ] + tables
    vmem = pl.BlockSpec(memory_space=pltpu.VMEM)
    dma = pltpu.SemaphoreType.DMA
    zz, ll, point = pl.pallas_call(
        functools.partial(main_kernel, z),
        out_shape=[
            jax.ShapeDtypeStruct((z.R, 2 * z.LN), F32),
            jax.ShapeDtypeStruct((z.R, C), F32),
            jax.ShapeDtypeStruct((C, C), F32),
        ],
        in_specs=[vmem] * len(args),
        out_specs=[vmem] * 3,
        scratch_shapes=[
            pltpu.VMEM((z.L + 1, 128, z.Y), BF16),
            pltpu.VMEM((z.L, C, z.Y), F32),
            pltpu.VMEM((C, z.Y), BF16),
            pltpu.VMEM((C, z.Y), BF16),
            pltpu.VMEM((z.L, 2, C, 128), BF16),
            pltpu.VMEM((z.S, z.RP, z.LN), BF16),
            pltpu.VMEM((z.N, z.RP, z.LN), BF16),
            pltpu.VMEM((z.N, z.RP, z.LN), BF16),
            pltpu.VMEM((z.S, z.RP, z.LN), BF16),
            pltpu.VMEM((z.R, C), F32),
            pltpu.VMEM((z.R, 2 * z.LN), F32),
            pltpu.VMEM((z.L, C, C), BF16),
            pltpu.VMEM((z.N, C, C), BF16),
            dma((z.S,)),
            dma((z.N,)),
            dma((z.N,)),
            dma((z.S,)),
            dma((z.S,)),
            dma((z.N,)),
            dma((z.L,)),
            dma((z.L,)),
        ],
        compiler_params=pltpu.CompilerParams(
            collective_id=0, has_side_effects=True, vmem_limit_bytes=VMEM_BYTES
        ),
        name="operator",
    )(*args)

    count = min(128 // z.RG, z.J)
    blocks = z.J // count
    grads = pl.pallas_call(
        functools.partial(outer_kernel, z, count),
        grid=(z.H, blocks),
        out_shape=jax.ShapeDtypeStruct((owned, kx, 2, C, C), F32),
        in_specs=[
            pl.BlockSpec((count * z.RG, 2 * z.LN), lambda h, j: (h * blocks + j, 0)),
            pl.BlockSpec((count * z.RG, C), lambda h, j: (h * blocks + j, 0)),
        ],
        out_specs=pl.BlockSpec((z.ML, count, 2, C, C), lambda h, j: (h, j, 0, 0, 0)),
        compiler_params=pltpu.CompilerParams(vmem_limit_bytes=VMEM_BYTES),
        name="outer",
    )(zz, ll)
    return grads[None], point[None]


def solution(mesh):
    in_specs = (
        P("groups", "space", None, None),
        P("groups", "space", None),
        P(),
        P(),
        P("segment", None, None),
        P("segment", None),
        P("segment", "space", None, None, None, None),
        P(),
        P(),
        P(),
    )
    out_specs = (
        P(("groups", "segment"), "space", None, None, None, None),
        P(("groups", "segment"), None, None),
    )
    return jax.shard_map(
        on_device, mesh=mesh, in_specs=in_specs, out_specs=out_specs, check_vma=False
    )
```

time: 621 us -> 102 us (0.16)
  the two profiles are of different devices: /device:TPU:3 before, /device:TPU:0 now
where the time goes in v1:
time: 102 us; the launch traced here: 101 us
  Pallas kernels  84.8 us (83%)
  local copies, waits for them, and re-layouts  12.7 us (12%)
  other arithmetic  2.77 us (3%)
    pallas_call x1, Pallas kernels, on_device(): pl.pallas_call(functools.partial(main_kernel, z), out_shape=[jax.ShapeDty...  80.4 us
    unnamed x19, local copies, waits for them, and re-layouts  9.46 us
    pallas_call x1, Pallas kernels, on_device(): pl.pallas_call(functools.partial(outer_kernel, z, count), grid=(z.H, bloc...  4.34 us

profile of v1, /device:TPU:0, one launch (start us, length us, event | category | flops | bytes accessed | tf_op | source)
XLA Modules:
  0.0 100.9 jit_solution(2352525554386952290)
XLA Ops:
  0.6 0.7 bitcast_convert_fusion
  1.3 0.7 fusion
  1.9 0.7 bitcast_convert_fusion.1
  2.6 0.1 pad.6.clone
  2.7 0.7 reshape.45.cotangent
  3.4 0.8 copy.20
  4.2 0.7 pad_bitcast_fusion
  4.9 0.8 maximum_bitcast_fusion
  5.7 0.1 copy.21
  5.8 0.7 copy.23.lift_b
  6.6 0.8 copy.22
  7.4 0.1 copy.25.out_w
  7.5 0.8 copy.24.proj_b
  8.3 0.9 copy-done
  9.2 0.9 copy-done.1
  10.2 0.9 copy-done.2
  11.1 0.9 copy-done.3
  12.1 0.9 copy-done.4
  13.0 0.9 copy-done.5
  14.0 0.8 copy-done.6
  14.8 0.7 copy-done.7
  15.5 80.4 %operator.1 = (f32[512,256]{1,0:T(8,128)S(1)}, f32[512,64]{1,0:T(8,128)S(1)}, f32[64,64]{1,0:T(8,128)S(1)}) custom-call(bf16[16,8,256]{2,1,0:T(8,128)(2,1)S(1)} %bitcast.26, f32[16,1,256]{2,1,0:T(1,128)S(1)} %reshape.45.cotangent, bf16[64,8]{1,0:T(8,128)(2,1)S(1)} %bitcast.27, f32[64,1]{1,0:T(8,128)S(1)} %copy.23.lift_b, ...), custom_call_target="tpu_custom_call" | custom-call | tf_op jit(solution)/shard_map/operator/pallas_call | solution.py:371
  96.0 4.3 %outer.1 = f32[4,32,2,64,64]{4,3,2,1,0:T(8,128)} custom-call(f32[512,256]{1,0:T(8,128)S(1)} %get-tuple-element.5.zz, f32[512,64]{1,0:T(8,128)S(1)} %get-tuple-element.6.ll), custom_call_target="tpu_custom_call" | custom-call | tf_op jit(solution)/shard_map/outer/pallas_call | solution.py:411
  100.3 0.6 copy.27
  (10 shorter events, 0.0 us)
Async XLA Ops:
  8.3 0.9 copy-start
  9.2 0.9 copy-start.1
  10.2 0.9 copy-start.2
  11.1 0.9 copy-start.3
  12.1 0.9 copy-start.4
  13.0 0.9 copy-start.5
  14.0 0.8 copy-start.6
  14.8 0.7 copy-start.7

commit v2 on v1

--- a/solution.py
+++ b/solution.py
@@ -13,7 +13,7 @@
 MESH = pl.DeviceIdType.MESH
 F32 = jnp.float32
 BF16 = jnp.bfloat16
-VMEM_BYTES = 48 * 1024 * 1024
+VMEM_BYTES = 63 * 1024 * 1024
 
 
 def dot(a, b, dims=((1,), (0,))):
@@ -58,7 +58,6 @@
     u = 2 * math.pi * ((f[:, None] * np.arange(nx)[None, :]) % nx) / nx
     c, s = np.cos(u) / math.sqrt(nx), np.sin(u) / math.sqrt(nx)
     fx = np.stack([np.stack([c, s], -1), np.stack([-s, c], -1)], 1)
-    ix = np.stack([np.stack([c.T, -s.T], -1), np.stack([s.T, c.T], -1)], 1)
 
     ytab = []
     for table in (fy, iy):
@@ -73,7 +72,7 @@
         ytab.append(out.reshape(z.ML * z.S * z.RP, z.Y))
 
     x1 = np.zeros((z.H, z.J, z.RG, z.N, z.RP))
-    x2, xg = np.zeros_like(x1), np.zeros_like(x1)
+    x2 = np.zeros_like(x1)
     for g in range(z.L):
         for sp in range(z.S):
             for un in range(z.U):
@@ -87,10 +86,9 @@
                             at = g * z.S + sp
                             for q in range(2):
                                 x1[h, :, r + q, at, col] = fx[:, q, x, p]
-                                xg[h, :, r + q, at, col] = ix[x, p, :, q]
                             x2[h, :, r, at, col] = -fx[:, 1, x, p]
                             x2[h, :, r + 1, at, col] = fx[:, 0, x, p]
-    xs = [a.reshape(z.R, z.K) for a in (x1, x2, xg)]
+    xs = [a.reshape(z.R, z.K) for a in (x1, x2)]
     tables = ytab + xs + [a.T for a in xs]
     return [np.ascontiguousarray(a).astype(ml_dtypes.bfloat16) for a in tables]
 
@@ -110,9 +108,11 @@
 
 
 def main_kernel(
-    z, inputs, cotangent, lift_wt, lift_b, pack_own, weights, proj_w, proj_wt, proj_b, out_w,
-    yf, yi, x1, x2, xg, x1t, x2t, xgt,
+    z, inputs_hbm, cotangent_hbm, lift_w_hbm, lift_b_hbm, point_hbm, bias_hbm, weights_hbm,
+    proj_w_hbm, proj_b_hbm, out_w_hbm, yf_hbm, yi_hbm, x1_hbm, x2_hbm, x1t_hbm, x2t_hbm,
     zz_out, ll_out, pg_out,
+    inputs, cotangent, lift_w, lift_b, point, bias, weights,
+    proj_w, proj_b, out_w, yf, yi, x1, x2, x1t, x2t, targets, in_sem,
     acts, slopes, pregrad, grad, pack, msg, recv, omsg, back, modes, spread, pgs, pgr,
     to_send, to_recv, back_send, back_recv, pg_send, pg_recv, gat_send, gat_recv,
 ):
@@ -124,14 +124,33 @@
     def device(g, s):
         return {"segment": g, "space": s}
 
-    def greet(i):
-        @pl.when(i != me)
-        def _():
-            pl.semaphore_signal(
-                barrier, inc=1, device_id=device(i // z.S, i % z.S), device_id_type=MESH
-            )
-
-    each(z.N, greet)
+    def greet(d):
+        i = (me + 1 + d) % z.N
+        pl.semaphore_signal(
+            barrier, inc=1, device_id=device(i // z.S, i % z.S), device_id_type=MESH
+        )
+
+    each(z.N - 1, greet)
+
+    def fetch(k, src, dst):
+        copy = pltpu.make_async_copy(src, dst, in_sem.at[k])
+        copy.start()
+        return copy
+
+    first = [(inputs_hbm, inputs), (lift_w_hbm, lift_w), (lift_b_hbm, lift_b), (yf_hbm, yf)]
+    second = [(point_hbm, point), (bias_hbm, bias), (yi_hbm, yi), (cotangent_hbm, cotangent)]
+    second += [(proj_w_hbm, proj_w), (proj_b_hbm, proj_b), (out_w_hbm, out_w)]
+    third = [(x1_hbm, x1), (x2_hbm, x2), (weights_hbm, weights), (x1t_hbm, x1t), (x2t_hbm, x2t)]
+    pairs = first + second + third
+    copies = [fetch(k, src, dst) for k, (src, dst) in enumerate(pairs)]
+    third_copies = copies[len(first) + len(second) :]
+
+    def column(row):
+        n = row.shape[1]
+        eye = lax.broadcasted_iota(jnp.int32, (n, n), 0) == lax.broadcasted_iota(
+            jnp.int32, (n, n), 1
+        )
+        return jnp.sum(jnp.where(eye, row, 0.0), axis=1, keepdims=True)
 
     def remote(src, dst, send, receive, g, s):
         return pltpu.make_async_remote_copy(
@@ -164,48 +183,53 @@
         )
 
     def pack_copy(g):
-        return remote(pack_own, pack.at[seg], gat_send.at[g], gat_recv.at[seg], g, sp)
+        return remote(pack.at[seg], pack.at[seg], gat_send.at[g], gat_recv.at[seg], g, sp)
 
     def pack_from(g):
-        return remote(pack_own, pack.at[g], gat_send.at[g], gat_recv.at[g], g, sp)
-
-    def other(g, s, act):
-        pl.when(jnp.logical_not((seg == g) & (sp == s)))(act)
+        return remote(pack.at[g], pack.at[g], gat_send.at[g], gat_recv.at[g], g, sp)
+
+    def owners(g, act):
+        pl.when(seg != g)(lambda: act(sp))
+        each(z.S - 1, lambda d: act((sp + 1 + d) % z.S))
+
+    def others(act):
+        each(z.N - 1, lambda d: act((me + 1 + d) % z.N))
 
     def send_rows(layer, table, values, wait_layer):
         co = dot(table[...], values, ((1,), (1,)))
         part = z.S * z.RP
         wide = jnp.concatenate([co[i * part : (i + 1) * part] for i in range(z.ML)], axis=1)
         if wait_layer is not None:
-            each(z.S, lambda s: other(wait_layer, s, lambda: to_copy(wait_layer, s).wait_send()))
+            owners(wait_layer, lambda s: to_copy(wait_layer, s).wait_send())
         msg[...] = wide.astype(BF16).reshape(z.S, z.RP, LN)
-        each(z.S, lambda s: other(layer, s, lambda: to_copy(layer, s).start()))
+        owners(layer, lambda s: to_copy(layer, s).start())
 
         @pl.when(seg == layer)
         def _():
             recv[me] = msg[sp]
 
     def received():
-        each(z.N, lambda i: pl.when(i != me)(lambda: from_copy(i).wait_recv()))
+        others(lambda i: from_copy(i).wait_recv())
         return recv[...].reshape(z.K, LN)
 
     def answer(rows):
         omsg[...] = rows.astype(BF16).reshape(z.N, z.RP, LN)
-        each(z.N, lambda i: pl.when(i != me)(lambda: back_copy(i).start()))
+        others(lambda i: back_copy(i).start())
         back[sp] = omsg[me]
 
     def answer_sent():
-        each(z.N, lambda i: pl.when(i != me)(lambda: back_copy(i).wait_send()))
+        others(lambda i: back_copy(i).wait_send())
 
     def answered(layer):
-        each(z.S, lambda s: other(layer, s, lambda: back_from(layer, s).wait_recv()))
+        owners(layer, lambda s: back_from(layer, s).wait_recv())
         rows = back[...].reshape(z.S * z.RP, LN)
         return jnp.concatenate([rows[:, i * C : (i + 1) * C] for i in range(z.ML)], axis=0)
 
     def own_part(value):
-        row = lax.broadcasted_iota(jnp.int32, value.shape, 0) % z.RG // Q
-        lane = lax.broadcasted_iota(jnp.int32, value.shape, 1) // C
-        return jnp.where(row == lane, value, 0.0)
+        row = lax.broadcasted_iota(jnp.int32, (z.RG, LN), 0) // Q
+        lane = lax.broadcasted_iota(jnp.int32, (z.RG, LN), 1) // C
+        grouped = value.reshape(z.R // z.RG, z.RG, LN)
+        return jnp.where((row == lane)[None], grouped, 0.0).reshape(z.R, LN)
 
     def kernel_of(i):
         h, j = i // z.J, i % z.J
@@ -221,19 +245,33 @@
     tail = jnp.where(tail < 2, 1.0, 0.0).astype(BF16)
     for layer in range(z.L):
         acts[layer, C:128, :] = tail
+    for copy in copies[: len(first)]:
+        copy.wait()
+    shift = column(lift_b[...])
     for u in range(z.U):
-        value = dot(lift_wt[...], inputs[seg * z.U + u]) + lift_b[...]
+        value = dot(lift_w[...], inputs[seg * z.U + u], ((0,), (0,))) + shift
         acts[0, 0:C, u * z.NY : (u + 1) * z.NY] = value.astype(BF16)
 
     pl.semaphore_wait(barrier, z.N - 1)
     send_rows(0, yf, acts[0, 0:C, :], None)
-    each(z.L, lambda g: pl.when(g != seg)(lambda: pack_copy(g).start()))
-    pack[seg] = pack_own[...]
-    each(z.L, lambda g: pl.when(g != seg)(lambda: pack_from(g).wait_recv()))
+
+    for copy in copies[len(first) : len(first) + len(second)]:
+        copy.wait()
+    wide = point[...].astype(F32)
+    high = bias[...].astype(BF16).astype(F32)
+    lane = lax.broadcasted_iota(jnp.int32, (C, 128 - C), 1)
+    side = jnp.where(lane == 0, column(high), jnp.where(lane == 1, column(bias[...] - high), 0.0))
+    pack[seg, 0] = jnp.concatenate([wide.T, side], axis=1).astype(BF16)
+    pack[seg, 1] = jnp.concatenate([wide, jnp.zeros_like(side)], axis=1).astype(BF16)
+    each(z.L - 1, lambda d: pack_copy((seg + 1 + d) % z.L).start())
+    targets[...] = cotangent[...].astype(F32).reshape(z.MB * z.rows, z.NY)
+    each(z.L - 1, lambda d: pack_from((seg + 1 + d) % z.L).wait_recv())
 
     def forward(layer, carry):
         @pl.when(seg == layer)
         def _():
+            for copy in third_copies:
+                copy.wait()
             got = received()
             zz_out[:, 0:LN] = own_part(dot(x1[...], got))
             zz_out[:, LN : 2 * LN] = own_part(dot(x2[...], got))
@@ -244,7 +282,7 @@
             each(z.H * z.J, mult)
             product = modes[...]
             product = own_part(jnp.concatenate([product] * z.ML, axis=1))
-            answer(dot(xgt[...], product.astype(BF16)))
+            answer(dot(x1t[...], product.astype(BF16)))
 
         local = dot(pack[layer, 0], acts[layer])
         pre = local + dot(answered(layer), yi[...], ((0,), (0,)))
@@ -261,9 +299,9 @@
     lax.fori_loop(0, z.L, forward, 0)
     answer_sent()
 
-    hidden = dot(proj_wt[...], acts[z.L, 0:C, :]) + proj_b[...]
-    target = jnp.concatenate([cotangent[seg * z.U + u] for u in range(z.U)], axis=1)
-    hidden_grad = (gelu_slope(hidden) * out_w[...] * target).astype(BF16)
+    hidden = dot(proj_w[...], acts[z.L, 0:C, :], ((0,), (0,))) + column(proj_b[...])
+    target = jnp.concatenate([targets[pl.ds(seg * z.U + u, 1), :] for u in range(z.U)], axis=1)
+    hidden_grad = (gelu_slope(hidden) * column(out_w[...]) * target).astype(BF16)
     grad[...] = dot(proj_w[...], hidden_grad).astype(BF16)
 
     def backward(step, carry):
@@ -273,18 +311,19 @@
 
         @pl.when(step > 0)
         def _():
-            each(z.S, lambda s: other(layer + 1, s, lambda: pg_copy(layer + 1, s).wait_send()))
+            owners(layer + 1, lambda s: pg_copy(layer + 1, s).wait_send())
 
         pgs[layer] = dot(acts[layer, 0:C, :], pregrad[...], ((1,), (1,))).astype(BF16)
-        each(z.S, lambda s: other(layer, s, lambda: pg_copy(layer, s).start()))
+        owners(layer, lambda s: pg_copy(layer, s).start())
 
         @pl.when(seg == layer)
         def _():
             pgr[me] = pgs[layer]
-            got = dot(xg[...], received())
+            got = dot(x1[...], received())
             if z.ML > 1:
-                row = lax.broadcasted_iota(jnp.int32, (z.R, C), 0) % z.RG // Q
-                got = jnp.where(row == 0, got[:, 0:C], got[:, C : 2 * C])
+                row = lax.broadcasted_iota(jnp.int32, (z.RG, C), 0) < Q
+                halves = [a.reshape(z.R // z.RG, z.RG, C) for a in (got[:, 0:C], got[:, C : 2 * C])]
+                got = jnp.where(row[None], halves[0], halves[1]).reshape(z.R, C)
             ll_out[...] = got
 
             @pl.when(layer > 0)
@@ -308,19 +347,20 @@
 
     lax.fori_loop(0, z.L, backward, 0)
 
-    each(z.N, lambda i: pl.when(i != me)(lambda: pg_from(i).wait_recv()))
+    others(lambda i: pg_from(i).wait_recv())
     total = pgr[0].astype(F32)
     for i in range(1, z.N):
         total = total + pgr[i].astype(F32)
     pg_out[...] = total * (1.0 / math.sqrt(z.MB * z.rows * z.S * z.NY))
 
-    each(z.S, lambda s: other(0, s, lambda: pg_copy(0, s).wait_send()))
-    each(z.S, lambda s: other(0, s, lambda: to_copy(0, s).wait_send()))
+    owners(0, lambda s: pg_copy(0, s).wait_send())
+    owners(0, lambda s: to_copy(0, s).wait_send())
     pl.when(seg > 0)(answer_sent)
-    each(z.L, lambda g: pl.when(g != seg)(lambda: pack_copy(g).wait_send()))
-
-
-def outer_kernel(z, count, zz, ll, out):
+    each(z.L - 1, lambda d: pack_copy((seg + 1 + d) % z.L).wait_send())
+
+
+def outer_kernel(z, count, zz, ll, point, out, point_out):
+    point_out[...] = point[...]
     turned = zz[...].T.astype(BF16)
     grads = ll[...]
     row = lax.broadcasted_iota(jnp.int32, grads.shape, 0) // z.RG
@@ -340,32 +380,21 @@
     batch, rows, steps, cols = inputs.shape
     _, owned, kx, _, C, _ = spectral_weight.shape
     z = Sizes(batch, rows, cols, lax.axis_size("segment"), lax.axis_size("space"), owned, kx, C)
-    hid = proj_weight.shape[1]
     tables = [jnp.asarray(t) for t in make_tables(z)]
 
-    w = point_weight[0]
-    bias = layer_bias[0]
-    high = bias.astype(BF16)
-    low = (bias - high.astype(F32)).astype(BF16)
-    gap = jnp.zeros((C, 128 - C - 2), BF16)
-    pack = jnp.stack(
-        [
-            jnp.concatenate([w.T, high[:, None], low[:, None], gap], axis=1),
-            jnp.concatenate([w, jnp.zeros((C, 128 - C), BF16)], axis=1),
-        ]
-    )
     args = [
         inputs.reshape(batch * rows, steps, cols),
-        cotangent.astype(F32).reshape(batch * rows, 1, cols),
-        lift_weight.T,
-        lift_bias[:, None],
-        pack,
+        cotangent,
+        lift_weight,
+        lift_bias[None],
+        point_weight[0],
+        layer_bias,
         spectral_weight[0],
         proj_weight,
-        proj_weight.T,
-        proj_bias[:, None],
-        out_weight.astype(F32)[:, None],
+        proj_bias[None],
+        out_weight.astype(F32)[None],
     ] + tables
+    held = [pltpu.VMEM(a.shape, a.dtype) for a in args]
     vmem = pl.BlockSpec(memory_space=pltpu.VMEM)
     dma = pltpu.SemaphoreType.DMA
     zz, ll, point = pl.pallas_call(
@@ -375,9 +404,12 @@
             jax.ShapeDtypeStruct((z.R, C), F32),
             jax.ShapeDtypeStruct((C, C), F32),
         ],
-        in_specs=[vmem] * len(args),
+        in_specs=[pl.BlockSpec(memory_space=pltpu.HBM)] * len(args),
         out_specs=[vmem] * 3,
-        scratch_shapes=[
+        scratch_shapes=held
+        + [
+            pltpu.VMEM((batch * rows, cols), F32),
+            dma((len(args),)),
             pltpu.VMEM((z.L + 1, 128, z.Y), BF16),
             pltpu.VMEM((z.L, C, z.Y), F32),
             pltpu.VMEM((C, z.Y), BF16),
@@ -406,20 +438,27 @@
         name="operator",
     )(*args)
 
-    count = min(128 // z.RG, z.J)
+    count = min(64 // z.RG, z.J)
     blocks = z.J // count
-    grads = pl.pallas_call(
+    grads, point = pl.pallas_call(
         functools.partial(outer_kernel, z, count),
         grid=(z.H, blocks),
-        out_shape=jax.ShapeDtypeStruct((owned, kx, 2, C, C), F32),
+        out_shape=[
+            jax.ShapeDtypeStruct((owned, kx, 2, C, C), F32),
+            jax.ShapeDtypeStruct((C, C), F32),
+        ],
         in_specs=[
             pl.BlockSpec((count * z.RG, 2 * z.LN), lambda h, j: (h * blocks + j, 0)),
             pl.BlockSpec((count * z.RG, C), lambda h, j: (h * blocks + j, 0)),
+            pl.BlockSpec((C, C), lambda h, j: (0, 0)),
         ],
-        out_specs=pl.BlockSpec((z.ML, count, 2, C, C), lambda h, j: (h, j, 0, 0, 0)),
+        out_specs=[
+            pl.BlockSpec((z.ML, count, 2, C, C), lambda h, j: (h, j, 0, 0, 0)),
+            pl.BlockSpec((C, C), lambda h, j: (0, 0)),
+        ],
         compiler_params=pltpu.CompilerParams(vmem_limit_bytes=VMEM_BYTES),
         name="outer",
-    )(zz, ll)
+    )(zz, ll, point)
     return grads[None], point[None]
 
 

time: 102 us -> 89.2 us (0.87)
  local copies, waits for them, and re-layouts: 12.7 us -> 0 us
  Pallas kernels: 84.8 us -> 86.9 us
  other arithmetic: 2.77 us -> 1.17 us
    unnamed x19 -> x0, local copies, waits for them, and re-layouts: 9.46 us -> none
    pallas_call x1, Pallas kernels: 4.34 us -> 7.09 us  [on_device(): pl.pallas_call(functools.partial(outer_kernel, z, count), grid=(z.H, bloc...]
    broadcast_in_dim x4 -> x0, local copies, waits for them, and re-layouts: 1.63 us -> none  [the longest x1 0.77 us: on_device(): proj_bias[:, None]]
    convert_element_type x2 -> x0, other arithmetic: 1.31 us -> none  [the longest x1 0.66 us: on_device(): low = (bias - high.astype(F32)).astype(BF16)]
where the time goes in v2:
time: 89.2 us; the launch traced here: 88.8 us
  Pallas kernels  86.9 us (97%)
  other arithmetic  1.17 us (1%)
    pallas_call x1, Pallas kernels, on_device(): pl.pallas_call(functools.partial(main_kernel, z), out_shape=[jax.ShapeDty...  79.9 us
    pallas_call x1, Pallas kernels, on_device(): pl.pallas_call(functools.partial(outer_kernel, z, count), grid=(z.H, bloc...  7.09 us

profile of v2, /device:TPU:0, one launch (start us, length us, event | category | flops | bytes accessed | tf_op | source)
XLA Modules:
  0.0 88.8 jit_solution(1930097699308139323)
XLA Ops:
  0.6 1.2 %bitcast_convert_fusion.out_w_hbm = f32[1,128]{1,0:T(1,128)} fusion(bf16[128]{0:T(256)(128)(2,1)} %param.25), kind=kLoop, calls=%fused_computation | loop fusion | flops 128 | bytes 768 | tf_op jit(solution)/shard_map/broadcast_in_dim | solution.py:395
  1.8 79.9 %operator.1 = (f32[512,256]{1,0:T(8,128)}, f32[512,64]{1,0:T(8,128)}, f32[64,64]{1,0:T(8,128)}) custom-call(bf16[16,8,256]{2,1,0:T(8,128)(2,1)} %bitcast.11, bf16[2,8,256]{2,1,0:T(8,128)(2,1)} %cotangent_hbm.1, bf16[8,64]{1,0:T(8,128)(2,1)} %lift_w_hbm.1, f32[1,64]{1,0:T(1,128)} %bitcast.13, bf16[64,64]{1,0:T(8,128)(2,1)} %bitcast.12, f32[1,64]{1,0:T(1,128)} %bias_hbm.1, ...), custom_call_target="tpu_custom_call" | custom-call | tf_op jit(solution)/shard_map/operator/pallas_call | solution.py:400
  81.7 7.1 %outer.1 = (f32[4,32,2,64,64]{4,3,2,1,0:T(8,128)}, f32[64,64]{1,0:T(8,128)}) custom-call(f32[512,256]{1,0:T(8,128)} %get-tuple-element.7.zz, f32[512,64]{1,0:T(8,128)} %get-tuple-element.8.ll, f32[64,64]{1,0:T(8,128)} %get-tuple-element.9.point), custom_call_target="tpu_custom_call" | custom-call | tf_op jit(solution)/shard_map/outer/pallas_call | solution.py:443

commit v3 on v2

--- a/solution.py
+++ b/solution.py
@@ -130,8 +130,6 @@
             barrier, inc=1, device_id=device(i // z.S, i % z.S), device_id_type=MESH
         )
 
-    each(z.N - 1, greet)
-
     def fetch(k, src, dst):
         copy = pltpu.make_async_copy(src, dst, in_sem.at[k])
         copy.start()
@@ -143,6 +141,7 @@
     third = [(x1_hbm, x1), (x2_hbm, x2), (weights_hbm, weights), (x1t_hbm, x1t), (x2t_hbm, x2t)]
     pairs = first + second + third
     copies = [fetch(k, src, dst) for k, (src, dst) in enumerate(pairs)]
+    each(z.N - 1, greet)
     third_copies = copies[len(first) + len(second) :]
 
     def column(row):
@@ -301,7 +300,7 @@
 
     hidden = dot(proj_w[...], acts[z.L, 0:C, :], ((0,), (0,))) + column(proj_b[...])
     target = jnp.concatenate([targets[pl.ds(seg * z.U + u, 1), :] for u in range(z.U)], axis=1)
-    hidden_grad = (gelu_slope(hidden) * column(out_w[...]) * target).astype(BF16)
+    hidden_grad = (gelu_slope(hidden) * column(out_w[...].astype(F32)) * target).astype(BF16)
     grad[...] = dot(proj_w[...], hidden_grad).astype(BF16)
 
     def backward(step, carry):
@@ -392,7 +391,7 @@
         spectral_weight[0],
         proj_weight,
         proj_bias[None],
-        out_weight.astype(F32)[None],
+        out_weight[None],
     ] + tables
     held = [pltpu.VMEM(a.shape, a.dtype) for a in args]
     vmem = pl.BlockSpec(memory_space=pltpu.VMEM)
@@ -438,7 +437,7 @@
         name="operator",
     )(*args)
 
-    count = min(64 // z.RG, z.J)
+    count = min(128 // z.RG, z.J)
     blocks = z.J // count
     grads, point = pl.pallas_call(
         functools.partial(outer_kernel, z, count),

time: 89.2 us -> 86.5 us (0.970)
  Pallas kernels: 86.9 us -> 85.7 us
  other arithmetic: 1.17 us -> 0 us
    pallas_call x1, Pallas kernels: 7.09 us -> 5.67 us  [on_device(): pl.pallas_call(functools.partial(outer_kernel, z, count), grid=(z.H, bloc...]
    broadcast_in_dim x1 -> x0, other arithmetic: 1.17 us -> none  [on_device(): out_weight.astype(F32)[None]]
where the time goes in v3:
time: 86.5 us; the launch traced here: 86.3 us
  Pallas kernels  85.7 us (99%)
    pallas_call x1, Pallas kernels, on_device(): pl.pallas_call(functools.partial(main_kernel, z), out_shape=[jax.ShapeDty...  80 us
    pallas_call x1, Pallas kernels, on_device(): pl.pallas_call(functools.partial(outer_kernel, z, count), grid=(z.H, bloc...  5.67 us

profile of v3, /device:TPU:0, one launch (start us, length us, event | category | flops | bytes accessed | tf_op | source)
XLA Modules:
  0.0 86.3 jit_solution(13244755272339035426)
XLA Ops:
  0.6 80.0 %operator.1 = (f32[512,256]{1,0:T(8,128)}, f32[512,64]{1,0:T(8,128)}, f32[64,64]{1,0:T(8,128)}) custom-call(bf16[16,8,256]{2,1,0:T(8,128)(2,1)} %bitcast.9, bf16[2,8,256]{2,1,0:T(8,128)(2,1)} %cotangent_hbm.1, bf16[8,64]{1,0:T(8,128)(2,1)} %lift_w_hbm.1, f32[1,64]{1,0:T(1,128)} %bitcast.11, bf16[64,64]{1,0:T(8,128)(2,1)} %bitcast.10, f32[1,64]{1,0:T(1,128)} %bias_hbm.1, ...), custom_call_target="tpu_custom_call" | custom-call | tf_op jit(solution)/shard_map/operator/pallas_call | solution.py:399
  80.7 5.7 %outer.1 = (f32[4,32,2,64,64]{4,3,2,1,0:T(8,128)}, f32[64,64]{1,0:T(8,128)}) custom-call(f32[512,256]{1,0:T(8,128)} %get-tuple-element.7.zz, f32[512,64]{1,0:T(8,128)} %get-tuple-element.8.ll, f32[64,64]{1,0:T(8,128)} %get-tuple-element.9.point), custom_call_target="tpu_custom_call" | custom-call | tf_op jit(solution)/shard_map/outer/pallas_call | solution.py:442
